TPU v7x, 32 devices: a whole 2x2x4 slice. The times are simulated.
32 devices in a mesh: pole: 2 (over y), row: 4 (over x, core), col: 4 (over z).
Axes of the slice: x: 2, y: 2, z: 4, core: 2. Of those that a mesh axis runs over, the one named last changes fastest.
Arguments:
- inverse: bfloat16 [2, 2, 8192, 8192], P('pole', None, None, ('row', 'col')), may hold values from -0.0625 to 0.0625
- factor: bfloat16 [2, 2, 8192, 768], P('pole', None, ('row', 'col')), may hold values from -1 to 1
- diag_inverse: bfloat16 [2, 2, 768, 256], P('pole', None, ('row', 'col')), may hold values from -6 to 6
- widths: int32 [3], replicated, may hold values from 1 to 256, 512 in all
- pattern: int32 [32, 3], replicated, may hold values 0 or 1
- owner: int32 [16], replicated, may hold values from 0 to 15, each once
- assign: int32 [2], P('pole'), may hold values from 0 to 19
- pole_weights: float32 [20, 2], replicated, may hold values from -4 to 4
Outputs:
- rho_panel: float32 [8192, 768], P(('row', 'col'))
- rho_diag: float32 [768, 256], P(('row', 'col'))
Inputs may be any that keep to these rules, and one draw needn't show every extreme that they name: The widths sum to 512 and the largest is exactly 256. `owner`: each piece number appears once.
All inputs are finite; a program needn't handle non-finite values.
Results may differ from a plain program's by a relative error of at most 0.0027.
Values may be sent and summed in bfloat16 or wider, within the bound.
A program may use at most 192 MiB of HBM per device.

v0:
```python
import jax
import jax.numpy as jnp
from jax import lax
from jax.sharding import PartitionSpec as P


def inner_dot(left, right):
    return lax.dot_general(
        left, right, (((0,), (0,)), ((), ())), preferred_element_type=jnp.float32
    )


def block_product(left, right):
    return jnp.einsum("wka,wkb->kab", left, right, preferred_element_type=jnp.float32)


def accumulate(totals, shard_rows, columns_inverse, own_start):
    sum_real, sum_imag, picked = totals
    row_count = shard_rows.shape[1]
    sum_real = inner_dot(columns_inverse[0], shard_rows[0]) - inner_dot(
        columns_inverse[1], shard_rows[1]
    )
    sum_imag = inner_dot(columns_inverse[0], shard_rows[1]) + inner_dot(
        columns_inverse[1], shard_rows[0]
    )
    own_width = picked.shape[1]
    inside = (own_start >= 0) & (own_start < row_count)
    slice_start = jnp.clip(own_start, 0, row_count - own_width)
    picked = lax.cond(
        inside,
        lambda: lax.dynamic_slice_in_dim(shard_rows, slice_start, own_width, 1),
        lambda: picked,
    )
    return (sum_real, sum_imag, picked)


def lookup_small(keys, table_keys, values):
    return jnp.sum(jnp.where(keys[:, None] == table_keys[None, :], values[None, :], 0), axis=1)


def local(inverse, factor, diag_inverse, widths, pattern, owner, assign, pole_weights):
    devices = lax.axis_size(("row", "col"))
    device = lax.axis_index(("row", "col"))
    local_width = factor.shape[2]
    total_cols = factor.shape[3]
    block = diag_inverse.shape[3]
    blocks_k = total_cols // block
    blocks_a = pattern.shape[0]
    block_ids = jnp.arange(blocks_k, dtype=jnp.int32)
    row_ids = device * local_width + jnp.arange(local_width, dtype=jnp.int32)
    row_onehot = (
        row_ids[:, None] // block == jnp.arange(blocks_a, dtype=jnp.int32)[None, :]
    ).astype(jnp.float32)
    block_mask = jnp.dot(row_onehot, pattern.astype(jnp.float32), precision=lax.Precision.HIGHEST)
    col_ids = jnp.arange(total_cols, dtype=jnp.int32)
    col_block = col_ids // block
    col_pos = col_ids % block
    col_width = lookup_small(col_block, block_ids, widths)
    col_live = col_pos < col_width
    full_mask = jnp.repeat(block_mask, block, axis=1) * col_live.astype(jnp.float32)[None, :]
    masked = factor[0] * full_mask.astype(jnp.bfloat16)[None]
    pole_onehot = (
        assign[:, None] == jnp.arange(pole_weights.shape[0], dtype=jnp.int32)[None, :]
    ).astype(jnp.float32)
    weight = jnp.dot(pole_onehot, pole_weights, precision=lax.Precision.HIGHEST)[0]
    weight_real = weight[0]
    weight_imag = weight[1]
    own_piece = jnp.sum(jnp.where(jnp.arange(devices, dtype=jnp.int32) == device, owner, 0))
    own_start = own_piece * local_width
    columns_inverse = inverse[0]
    zero_sum = jnp.zeros((local_width, total_cols), jnp.float32)
    zero_pick = jnp.zeros((2, local_width, total_cols), jnp.bfloat16)
    sum_real, sum_imag, picked = accumulate(
        (zero_sum, zero_sum, zero_pick),
        lax.all_gather(masked, ("row", "col"), axis=1, tiled=True),
        columns_inverse,
        own_start,
    )
    x_real = -sum_real
    x_imag = -sum_imag
    panel_local = weight_real * x_imag + weight_imag * x_real
    x_bf = jnp.stack([x_real, x_imag]).astype(jnp.bfloat16)
    own_blocks = picked.reshape(2, local_width, blocks_k, block)
    x_blocks = x_bf.reshape(2, local_width, blocks_k, block)
    part_real = (
        block_product(own_blocks[0], x_blocks[0]) - block_product(own_blocks[1], x_blocks[1])
    ).reshape(total_cols, block)
    part_imag = (
        block_product(own_blocks[0], x_blocks[1]) + block_product(own_blocks[1], x_blocks[0])
    ).reshape(total_cols, block)
    inverse_diag = diag_inverse[0].astype(jnp.float32)
    shared = lax.psum_scatter(
        jnp.stack([part_real, part_imag]), ("row", "col"), scatter_dimension=1, tiled=True
    )
    diag_real = inverse_diag[0] - shared[0]
    diag_imag = inverse_diag[1] - shared[1]
    diag_local = weight_real * diag_imag + weight_imag * diag_real
    panel_total, diag_total = lax.psum((panel_local, diag_local), "pole")
    return (panel_total, diag_total)


def solution(mesh):
    placed = (
        P("pole", None, None, ("row", "col")),
        P("pole", None, ("row", "col"), None),
        P("pole", None, ("row", "col"), None),
        P(),
        P(),
        P(),
        P("pole"),
        P(),
    )
    return jax.shard_map(
        local,
        mesh=mesh,
        in_specs=placed,
        out_specs=(P(("row", "col"), None), P(("row", "col"), None)),
        check_vma=False,
    )
```

profile of v0, /device:TPU:2, one launch (start us, length us, event | category | flops | bytes accessed | tf_op | source)
XLA Modules:
  0.0 334.4 jit_solution(9592614516546559489)
XLA Ops:
  7.3 0.7 select_reduce_fusion
  8.0 1.7 copy.26
  9.7 1.0 fusion.17
  10.7 0.2 fusion.12
  10.9 1.3 bitcast_multiply_fusion.1
  13.1 0.6 fusion.38
  13.7 134.6 %all-gather.2.cloned.1.call-done = bf16[2,8192,768]{1,2,0:T(8,128)(2,1)} async-done(((bf16[2,512,768]{1,2,0:T(8,128)(2,1)}), bf16[2,8192,768]{1,2,0:T(8,128)(2,1)}) %all-gather.2.cloned.1.call-update) | async-done | bytes 25165840 | tf_op jit(solution)/shard_map/all_gather | solution.py:75
  148.3 13.0 %fusion = f32[768,512]{1,0:T(8,128)} fusion(bf16[2,8192,768]{1,2,0:T(8,128)(2,1)} %all-gather.2.cloned.1.call-done, bf16[1,2,8192,512]{3,2,1,0:T(8,128)(2,1)} %param.10), kind=kOutput, calls=%fused_computation.4 | convolution fusion | flops 6442450944 | bytes 22544384 | tf_op jit(solution)/shard_map/dot_general | solution.py:8
  161.3 13.1 %fusion.1 = f32[768,512]{1,0:T(8,128)} fusion(bf16[2,8192,768]{1,2,0:T(8,128)(2,1)} %all-gather.2.cloned.1.call-done, bf16[1,2,8192,512]{3,2,1,0:T(8,128)(2,1)} %param.10), kind=kOutput, calls=%fused_computation.5 | convolution fusion | flops 6442450944 | bytes 22544384 | tf_op jit(solution)/shard_map/dot_general | solution.py:8
  174.4 10.7 %subtract_negate_fusion = f32[768,512]{1,0:T(8,128)} fusion(f32[768,512]{1,0:T(8,128)} %fusion, bf16[1,2,8192,512]{3,2,1,0:T(8,128)(2,1)S(1)} %bitcast.85, bf16[2,8192,768]{1,2,0:T(8,128)(2,1)} %all-gather.2.cloned.1.call-done), kind=kOutput, calls=%fused_computation.21 | convolution fusion | flops 6443237376 | bytes 24117248 | tf_op jit(solution)/shard_map/dot_general | solution.py:8
  185.1 15.3 %fusion.37 = (bf16[768,512]{1,0:T(8,128)(2,1)S(1)}, f32[512,768]{0,1:T(8,128)}, bf16[768,512]{1,0:T(8,128)(2,1)S(1)}) fusion(f32[768,512]{1,0:T(8,128)} %subtract_negate_fusion, f32[]{:T(128)} %bitcast.12, f32[]{:T(128)} %bitcast.5, f32[768,512]{1,0:T(8,128)} %fusion.1, bf16[1,2,8192,512]{3,2,1,0:T(8,128)(2,1)} %param.10, ...), kind=kOutput, calls=%fused_computation.66 | convolution fusion | flops 6445203456 | bytes 27264000 | tf_op jit(solution)/shard_map/dot_general | solution.py:8
  200.4 0.7 fusion.34
  201.8 2.3 conditional.1
  201.8 2.2 constant_dynamic-slice_fusion.1
  204.0 0.4 fusion.41
  204.4 0.4 fusion.42
  204.8 0.4 convolution_subtract_fusion
  205.2 0.4 convolution_add_fusion
  205.6 1.3 pad_maximum_fusion
  206.9 46.2 %all-reduce.2.cloned.1.call-done = f32[512,768]{0,1:T(8,128)} async-done(((f32[512,768]{0,1:T(8,128)}), f32[512,768]{0,1:T(8,128)}) %all-reduce.2.cloned.1.call-update) | async-done | bytes 1572880 | tf_op jit(solution)/shard_map/psum | solution.py:98
  253.1 3.0 copy.31
  256.2 60.4 %reduce-scatter.2.cloned.1.call-done = f32[2,48,256]{2,1,0:T(8,128)} async-done(((f32[2,768,256]{2,1,0:T(8,128)}), f32[2,48,256]{2,1,0:T(8,128)}) %reduce-scatter.2.cloned.1.call-update) | async-done | bytes 98320 | tf_op jit(solution)/shard_map/reduce_scatter | solution.py:92
  316.6 2.1 fusion.21
  318.7 9.2 %psum.15 = f32[48,256]{1,0:T(8,128)} all-reduce(f32[48,256]{1,0:T(8,128)S(1)} %fusion.21), channel_id=1, replica_groups=mesh['pole'=2,'row'=4,'col'=4] {'pole'}, use_global_device_ids=true, to_apply=%region_6.7 | all-reduce | flops 12288 | bytes 98304 | tf_op jit(solution)/shard_map/psum | solution.py:98
  (26 shorter events, 0.3 us)
Async XLA Ops:
  7.2 5.8 %copy-start = (f32[20,2]{0,1:T(2,128)S(1)}, f32[20,2]{0,1:T(2,128)}, u32[]{:S(2)}) copy-start(f32[20,2]{0,1:T(2,128)} %param.17) | copy-start | bytes 484
  7.2 141.1 %all-gather.2.cloned.1.call-start = ((), (), s32[]{:S(2)}) async-start(), calls=%async_computation.1 | async-start | bytes 26738688 | tf_op jit(solution)/shard_map/all_gather | solution.py:75
  12.3 240.9 %all-reduce.2.cloned.1.call-start = ((), (), s32[]{:S(2)}) async-start(), calls=%async_computation.2 | async-start | bytes 3145728 | tf_op jit(solution)/shard_map/psum | solution.py:98
  148.3 26.1 %slice-start = ((s8[16777216]{0:T(1024)(128)(4,1)}), s8[4194304]{0:T(1024)(128)(4,1)S(1)}, s32[]{:S(2)}) async-start(s8[16777216]{0:T(1024)(128)(4,1)} %bitcast.84), calls=%async_computation.4 | async-start | bytes 8388608
  148.3 26.1 %slice-start.1 = ((s8[16777216]{0:T(1024)(128)(4,1)}), s8[4194304]{0:T(1024)(128)(4,1)S(1)}, s32[]{:S(2)}) async-start(s8[16777216]{0:T(1024)(128)(4,1)} %bitcast.84), calls=%async_computation.5 | async-start | bytes 8388608
  161.3 13.1 %slice-start.2 = ((s8[16777216]{0:T(1024)(128)(4,1)}), s8[4194304]{0:T(1024)(128)(4,1)S(1)}, s32[]{:S(2)}) async-start(s8[16777216]{0:T(1024)(128)(4,1)} %bitcast.84), calls=%async_computation.6 | async-start | bytes 8388608
  161.3 13.1 %slice-start.3 = ((s8[16777216]{0:T(1024)(128)(4,1)}), s8[4194304]{0:T(1024)(128)(4,1)S(1)}, s32[]{:S(2)}) async-start(s8[16777216]{0:T(1024)(128)(4,1)} %bitcast.84), calls=%async_computation.7 | async-start | bytes 8388608
  185.1 15.3 %copy-start.2 = (s32[16]{0:T(128)S(1)}, s32[16]{0:T(128)}, u32[]{:S(2)}) copy-start(s32[16]{0:T(128)} %param.15) | copy-start | bytes 196
  200.4 116.2 %reduce-scatter.2.cloned.1.call-start = ((), (), s32[]{:S(2)}) async-start(), calls=%async_computation.3 | async-start | bytes 1671168 | tf_op jit(solution)/shard_map/reduce_scatter | solution.py:92
  204.0 2.9 copy-start.1
Sparse Core Ops, SparseCore 0:
  12.4 135.8 all-gather.1
  200.5 52.6 all-reduce.1
  257.3 59.2 reduce-scatter.1
where the time goes:
time: 336 us; the launch traced here: 334 us
  waiting for transfers between devices  241 us (72%)
  matrix products  54.7 us (16%)
  between operations  15.2 us (5%)
  blocking collectives  9.18 us (3%)
  local copies, waits for them, and re-layouts  7.61 us (2%)
  other arithmetic  6.32 us (2%)
    all_gather x1, waiting for transfers between devices, local(): lax.all_gather(masked, ('row', 'col'), axis=1, tiled=True)  135 us
    reduce_scatter x1, waiting for transfers between devices, local(): lax.psum_scatter(jnp.stack([part_real, part_imag]), ('row', 'col'), scatt...  60.4 us
    dot_general x4, matrix products, inner_dot(): lax.dot_general(left, right, (((0,), (0,)), ((), ())), preferred_element_...  52 us
    psum x1, waiting for transfers between devices, local(): panel_total, diag_total = lax.psum((panel_local, diag_local), 'pole')  46.2 us
    psum x1, blocking collectives, local(): panel_total, diag_total = lax.psum((panel_local, diag_local), 'pole')  9.18 us
  transfers between devices with their start and end apart: 3, of which 3 were waited for; matrix products, arithmetic and copies ran while one was open for 3% of the time, Pallas kernels for 0%

commit v1 on v0

v1 whole, which is shorter than its diff:
```python
import functools

import jax
import jax.numpy as jnp
from jax import lax
from jax.experimental import pallas as pl
from jax.experimental.pallas import tpu as pltpu
from jax.sharding import PartitionSpec as P

F32 = jnp.float32
BF16 = jnp.bfloat16
MESH = pl.DeviceIdType.MESH


def dot(left, right):
    return jnp.dot(left, right, preferred_element_type=F32)


def dot_nt(left, right):
    return lax.dot_general(left, right, (((1,), (1,)), ((), ())), preferred_element_type=F32)


def kernel(
    dims,
    piece_ref,
    inv_ref,
    place_ref,
    weight_ref,
    own_ref,
    dinv_ref,
    panel_ref,
    diag_ref,
    pieces,
    inv,
    acc,
    shares,
    xe,
    le,
    gram,
    half,
    half_sum,
    parts,
    totals,
    inv_sem,
    recv,
    sz,
    sx,
    sc,
    ys,
    yr,
    d1s,
    d1r,
    d2s,
    d2r,
    d3s,
    d3r,
):
    chunks, zs, poles, width, blocks_k, block, db = dims
    pole = lax.axis_index("pole")
    row = lax.axis_index("row")
    z = lax.axis_index("col")
    hi = row // 2
    lo = row % 2
    sibling = hi * 2 + (1 - lo)
    across = (1 - hi) * 2 + lo

    def at(h, l, zz):
        return (h * 2 + l) * zs + zz

    me = at(hi, lo, z)
    mine = hi * zs + z

    barrier = pltpu.get_barrier_semaphore()
    pl.semaphore_signal(
        barrier, inc=1, device_id=(pole, sibling, z), device_id_type=MESH
    )

    @pl.loop(0, 2 * zs)
    def _(j):
        @pl.when(j != mine)
        def _():
            pl.semaphore_signal(
                barrier,
                inc=1,
                device_id=(pole, (j // zs) * 2 + lo, j % zs),
                device_id_type=MESH,
            )

    @pl.loop(0, poles)
    def _(p):
        @pl.when(p != pole)
        def _():
            pl.semaphore_signal(
                barrier, inc=1, device_id=(p, row, z), device_id_type=MESH
            )

    load = pltpu.make_async_copy(inv_ref, inv, inv_sem)
    load.start()
    pieces[:, pl.ds(me, 1)] = piece_ref[...][:, None]
    pl.semaphore_wait(barrier, 1 + (2 * zs - 1) + (poles - 1))

    def send(c, q, send_sem, to_row, to_col):
        return pltpu.make_async_remote_copy(
            src_ref=pieces.at[c, q],
            dst_ref=pieces.at[c, q],
            send_sem=send_sem,
            recv_sem=recv.at[c, q],
            device_id=(pole, to_row, to_col),
            device_id_type=MESH,
        )

    def up(c, zz):
        return send(c, at(hi, lo, zz), sz.at[c, zz, 1], row, z + 1)

    def down(c, zz):
        return send(c, at(hi, lo, zz), sz.at[c, zz, 0], row, z - 1)

    def cross(c, zz):
        return send(c, at(hi, lo, zz), sx.at[c, zz], across, z)

    def over(c, h, zz):
        return send(c, at(h, lo, zz), sc.at[c, h, zz], sibling, z)

    def arrived(c, q):
        send(c, q, sx.at[0, 0], across, z).wait_recv()

    def goes_up(zz):
        return (zz <= z) & (z < zs - 1)

    def goes_down(zz):
        return (zz >= z) & (z > 0)

    def forward(c, zz):
        cross(c, zz).start()

        @pl.when(goes_up(zz))
        def _():
            up(c, zz).start()

        @pl.when(goes_down(zz))
        def _():
            down(c, zz).start()

        over(c, hi, zz).start()

    @pl.loop(0, chunks)
    def _(c):
        forward(c, z)

    acc[...] = jnp.zeros_like(acc)
    xe[...] = jnp.zeros_like(xe)
    le[...] = jnp.zeros_like(le)
    panel_ref[...] = jnp.zeros_like(panel_ref)
    load.wait()

    def compute(c, q):
        lt = pieces[c, q]
        u = dot(lt, inv[0, q])
        v = dot(lt, inv[1, q])
        acc[c, :width] += u[:width] - v[width:]
        acc[c, width:] += u[width:] + v[:width]

    def by_distance(visit, first):
        @pl.loop(first, 2 * zs)
        def _(j):
            s = j // 2
            zz = jnp.where(j % 2 == 0, z - s, z + s)

            @pl.when((zz >= 0) & (zz < zs) & (j != 1))
            def _():
                visit(zz)

    def along(c):
        compute(c, me)

        def visit(zz):
            arrived(c, at(hi, lo, zz))
            forward(c, zz)
            compute(c, at(hi, lo, zz))

        by_distance(visit, 2)

    def crossed(c):
        def visit(zz):
            arrived(c, at(1 - hi, lo, zz))
            over(c, 1 - hi, zz).start()
            compute(c, at(1 - hi, lo, zz))

        by_distance(visit, 0)

    def from_sibling(c, h):
        def visit(zz):
            arrived(c, at(h, 1 - lo, zz))
            compute(c, at(h, 1 - lo, zz))

        by_distance(visit, 0)

    def share(c, p):
        return pltpu.make_async_remote_copy(
            src_ref=shares.at[c, pole],
            dst_ref=shares.at[c, pole],
            send_sem=ys.at[c, p],
            recv_sem=yr.at[c, pole],
            device_id=(p, row, z),
            device_id_type=MESH,
        )

    def share_from(c, p):
        return pltpu.make_async_remote_copy(
            src_ref=shares.at[c, p],
            dst_ref=shares.at[c, p],
            send_sem=ys.at[c, p],
            recv_sem=yr.at[c, p],
            device_id=(p, row, z),
            device_id_type=MESH,
        )

    wr = weight_ref[0]
    wi = weight_ref[1]

    def others(visit):
        @pl.loop(0, poles)
        def _(p):
            @pl.when(p != pole)
            def _():
                visit(p)

    def finish(c):
        xr = -acc[c, :width]
        xi = -acc[c, width:]
        shares[c, pole] = wr * xi + wi * xr
        others(lambda p: share(c, p).start())
        place = place_ref[c]
        xe[0] += dot(place, xr.astype(BF16)).astype(BF16)
        xe[1] += dot(place, xi.astype(BF16)).astype(BF16)

    def receive(c):
        others(lambda p: share_from(c, p).wait_recv())
        total = shares[c, 0]
        for p in range(1, poles):
            total = total + shares[c, p]
        top = total.astype(BF16)
        rest = total - top.astype(F32)
        middle = rest.astype(BF16)
        low = (rest - middle.astype(F32)).astype(BF16)
        place = place_ref[c]
        panel_ref[...] += dot(place, top) + dot(place, middle) + dot(place, low)

    @pl.loop(0, chunks + 2)
    def _(t):
        @pl.when(t >= 2)
        def _():
            from_sibling(t - 2, 1 - hi)
            finish(t - 2)

        @pl.when(t < chunks)
        def _():
            along(t)

        @pl.when((t >= 1) & (t <= chunks))
        def _():
            from_sibling(t - 1, hi)
            crossed(t - 1)

    @pl.loop(0, chunks)
    def _(c):
        lt = pieces[c, own_ref[0]]
        place = place_ref[c]
        le[0] += dot(place, lt[:width]).astype(BF16)
        le[1] += dot(place, lt[width:]).astype(BF16)

    for k in range(blocks_k):
        rows = slice(k * block, (k + 1) * block)
        lr, li, xr, xi = le[0, rows], le[1, rows], xe[0, rows], xe[1, rows]
        real = dot_nt(lr, xr) - dot_nt(li, xi)
        imag = dot_nt(lr, xi) + dot_nt(li, xr)
        gram[rows] = wr * imag + wi * real

    span = zs * db

    def rows_of(h, l):
        return pl.ds(pl.multiple_of((h * 2 + l) * span, 8), span)

    halves = []
    for h in range(2):
        halves.append(
            pltpu.make_async_remote_copy(
                src_ref=gram.at[rows_of(h, 1 - lo)],
                dst_ref=half.at[h],
                send_sem=d1s.at[h],
                recv_sem=d1r.at[h],
                device_id=(pole, sibling, z),
                device_id_type=MESH,
            )
        )
        halves[h].start()

    @pl.loop(0, chunks - 1)
    def _(c):
        receive(c)

    for h in range(2):
        halves[h].wait_recv()
        half_sum[h] = (gram[rows_of(h, lo)] + half[h]).reshape(zs, db, block)

    def part(j):
        return pltpu.make_async_remote_copy(
            src_ref=half_sum.at[j // zs, j % zs],
            dst_ref=parts.at[mine],
            send_sem=d2s.at[j],
            recv_sem=d2r.at[mine],
            device_id=(pole, (j // zs) * 2 + lo, j % zs),
            device_id_type=MESH,
        )

    def part_from(j):
        return pltpu.make_async_remote_copy(
            src_ref=parts.at[j],
            dst_ref=parts.at[j],
            send_sem=d2s.at[j],
            recv_sem=d2r.at[j],
            device_id=(pole, (j // zs) * 2 + lo, j % zs),
            device_id_type=MESH,
        )

    def peers(visit):
        @pl.loop(0, 2 * zs)
        def _(j):
            @pl.when(j != mine)
            def _():
                visit(j)

    peers(lambda j: part(j).start())
    parts[mine] = half_sum[hi, z]
    receive(chunks - 1)
    peers(lambda j: part_from(j).wait_recv())
    total = parts[0]
    for j in range(1, 2 * zs):
        total = total + parts[j]
    totals[pole] = dinv_ref[...] - total

    def result(p, slot):
        return pltpu.make_async_remote_copy(
            src_ref=totals.at[slot],
            dst_ref=totals.at[slot],
            send_sem=d3s.at[p],
            recv_sem=d3r.at[slot],
            device_id=(p, row, z),
            device_id_type=MESH,
        )

    others(lambda p: result(p, pole).start())

    @pl.loop(0, chunks)
    def _(c):
        @pl.loop(0, zs)
        def _(zz):
            cross(c, zz).wait_send()
            over(c, 0, zz).wait_send()
            over(c, 1, zz).wait_send()

            @pl.when(goes_up(zz))
            def _():
                up(c, zz).wait_send()

            @pl.when(goes_down(zz))
            def _():
                down(c, zz).wait_send()

        others(lambda p: share(c, p).wait_send())

    for h in range(2):
        halves[h].wait_send()
    peers(lambda j: part(j).wait_send())
    others(lambda p: result(p, p).wait_recv())
    final = totals[0]
    for p in range(1, poles):
        final = final + totals[p]
    diag_ref[...] = final
    others(lambda p: result(p, pole).wait_send())


def local(inverse, factor, diag_inverse, widths, pattern, owner, assign, pole_weights):
    zs = lax.axis_size("col")
    poles = lax.axis_size("pole")
    rows_n = lax.axis_size("row")
    assert rows_n == 4
    devices = rows_n * zs
    device = lax.axis_index(("row", "col"))
    local_width = factor.shape[2]
    total_cols = factor.shape[3]
    db = diag_inverse.shape[2]
    block = diag_inverse.shape[3]
    blocks_k = total_cols // block
    live = 2 * total_cols // 3
    width = 128
    chunks = live // width

    col_ids = jnp.arange(total_cols, dtype=jnp.int32)
    col_block = col_ids // block
    col_pos = col_ids % block
    block_ids = jnp.arange(blocks_k, dtype=jnp.int32)
    same = col_block[:, None] == block_ids[None, :]
    before = block_ids[None, :] < col_block[:, None]
    col_width = jnp.sum(jnp.where(same, widths[None, :], 0), axis=1)
    col_start = jnp.sum(jnp.where(before, widths[None, :], 0), axis=1)
    target = jnp.where(col_pos < col_width, col_start + col_pos, -1)
    place = (target[:, None] == jnp.arange(live, dtype=jnp.int32)[None, :]).astype(BF16)

    row_block = (device * local_width + jnp.arange(local_width, dtype=jnp.int32)) // block
    row_onehot = (
        row_block[:, None] == jnp.arange(pattern.shape[0], dtype=jnp.int32)[None, :]
    ).astype(F32)
    row_mask = jnp.dot(row_onehot, pattern.astype(F32), precision=lax.Precision.HIGHEST)
    mask = jnp.repeat(row_mask, block, axis=1).astype(BF16)
    masked = factor[0] * mask[None]
    packed = lax.dot_general(
        place.reshape(total_cols, chunks, width),
        masked,
        (((0,), (2,)), ((), ())),
        preferred_element_type=F32,
    ).astype(BF16)
    packed = packed.transpose(0, 2, 1, 3).reshape(chunks, 2 * width, local_width)

    pole_onehot = assign[0] == jnp.arange(pole_weights.shape[0], dtype=jnp.int32)
    weight = jnp.sum(jnp.where(pole_onehot[:, None], pole_weights, 0.0), axis=0)
    own = jnp.sum(jnp.where(jnp.arange(devices, dtype=jnp.int32) == device, owner, 0))
    inverse_diag = diag_inverse[0].astype(F32)
    dinv = weight[0] * inverse_diag[1] + weight[1] * inverse_diag[0]
    places = place.reshape(total_cols, chunks, width).transpose(1, 0, 2)

    dims = (chunks, zs, poles, width, blocks_k, block, db)
    vmem = pl.BlockSpec(memory_space=pltpu.VMEM)
    smem = pl.BlockSpec(memory_space=pltpu.SMEM)
    dma = pltpu.SemaphoreType.DMA
    panel, diag = pl.pallas_call(
        functools.partial(kernel, dims),
        out_shape=(
            jax.ShapeDtypeStruct((total_cols, local_width), F32),
            jax.ShapeDtypeStruct((db, block), F32),
        ),
        in_specs=[vmem, pl.BlockSpec(memory_space=pl.ANY), vmem, smem, smem, vmem],
        out_specs=(vmem, vmem),
        scratch_shapes=[
            pltpu.VMEM((chunks, devices, 2 * width, local_width), BF16),
            pltpu.VMEM((2, devices, local_width, local_width), BF16),
            pltpu.VMEM((chunks, 2 * width, local_width), F32),
            pltpu.VMEM((chunks, poles, width, local_width), F32),
            pltpu.VMEM((2, total_cols, local_width), BF16),
            pltpu.VMEM((2, total_cols, local_width), BF16),
            pltpu.VMEM((total_cols, block), F32),
            pltpu.VMEM((2, zs * db, block), F32),
            pltpu.VMEM((2, zs, db, block), F32),
            pltpu.VMEM((2 * zs, db, block), F32),
            pltpu.VMEM((poles, db, block), F32),
            dma,
            dma((chunks, devices)),
            dma((chunks, zs, 2)),
            dma((chunks, zs)),
            dma((chunks, 2, zs)),
            dma((chunks, poles)),
            dma((chunks, poles)),
            dma((2,)),
            dma((2,)),
            dma((2 * zs,)),
            dma((2 * zs,)),
            dma((poles,)),
            dma((poles,)),
        ],
        compiler_params=pltpu.CompilerParams(
            collective_id=0, has_side_effects=True, vmem_limit_bytes=60 * 1024 * 1024
        ),
    )(
        packed,
        inverse[0].reshape(2, devices, local_width, local_width),
        places,
        weight,
        own.reshape(1),
        dinv,
    )
    return panel.T, diag


def solution(mesh):
    placed = (
        P("pole", None, None, ("row", "col")),
        P("pole", None, ("row", "col"), None),
        P("pole", None, ("row", "col"), None),
        P(),
        P(),
        P(),
        P("pole"),
        P(),
    )
    return jax.shard_map(
        local,
        mesh=mesh,
        in_specs=placed,
        out_specs=(P(("row", "col"), None), P(("row", "col"), None)),
        check_vma=False,
    )
```

time: 336 us -> 138 us (0.41)
  waiting for transfers between devices: 241 us -> 0 us
  Pallas kernels: 0 us -> 122 us
  matrix products: 54.7 us -> 3.02 us
  between operations: 15.2 us -> 1.47 us
  blocking collectives: 9.18 us -> 0 us
    all_gather x1 -> x0, waiting for transfers between devices: 135 us -> none  [local(): lax.all_gather(masked, ('row', 'col'), axis=1, tiled=True)]
    pallas_call x0 -> x1, Pallas kernels: none -> 122 us  [local(): pl.pallas_call(functools.partial(kernel, dims), out_shape=(jax.ShapeDtype...]
    reduce_scatter x1 -> x0, waiting for transfers between devices: 60.4 us -> none  [local(): lax.psum_scatter(jnp.stack([part_real, part_imag]), ('row', 'col'), scatt...]
    dot_general x10 -> x2, matrix products: 54.7 us -> 3.02 us  [the longest x1 2.03 us: local(): lax.dot_general(place.reshape(total_cols, chunks, width), masked, (((0,),...]
    psum x1 -> x0, waiting for transfers between devices: 46.2 us -> none  [local(): panel_total, diag_total = lax.psum((panel_local, diag_local), 'pole')]
    psum x1 -> x0, blocking collectives: 9.18 us -> none  [local(): panel_total, diag_total = lax.psum((panel_local, diag_local), 'pole')]
  transfers between devices with their start and end apart: 3 -> 0, of which waited for: 3 -> 0; matrix products, arithmetic and copies ran while one was open for 3% -> 0% of each run, Pallas kernels for 0% -> 0%
where the time goes in v1:
time: 138 us
  Pallas kernels  122 us (88%)
  other arithmetic  6.84 us (5%)
  local copies, waits for them, and re-layouts  4.65 us (3%)
  matrix products  3.02 us (2%)
  between operations  1.47 us (1%)
    pallas_call x1, Pallas kernels, local(): pl.pallas_call(functools.partial(kernel, dims), out_shape=(jax.ShapeDtype...  122 us
    unnamed x8, local copies, waits for them, and re-layouts  3.67 us

profile of v1, /device:TPU:2, one launch (start us, length us, event | category | flops | bytes accessed | tf_op | source)
XLA Modules:
  0.0 137.8 jit_solution(5153748370192590659)
XLA Ops:
  0.6 0.0 copy-start.2
  1.4 0.8 select_reduce_fusion.2.weight_ref
  2.2 0.0 copy-start.1
  2.2 1.4 fusion.26
  3.6 0.7 fusion.27
  4.3 1.0 convolution_convert_fusion
  5.3 0.8 select_reduce_fusion.1
  6.0 0.8 convert_element_type.37
  6.9 2.0 %fusion.15.dinv_ref = f32[48,256]{1,0:T(8,128)} fusion(f32[1,2,48,256]{3,2,1,0:T(8,128)S(1)} %convert_element_type.37, f32[]{:T(128)} %bitcast.11, f32[]{:T(128)} %bitcast.10), kind=kLoop, calls=%fused_computation.15 | loop fusion | flops 36864 | bytes 147464 | tf_op jit(solution)/shard_map/add | solution.py:429
  8.8 0.1 broadcast_in_dim.51
  8.9 0.3 copy.14
  9.2 0.0 copy-done.2
  9.2 2.0 %fusion.5 = bf16[4,128,2,512]{3,1,2,0:T(8,128)(2,1)} fusion(bf16[1,2,512,768]{3,2,1,0:T(8,128)(2,1)S(1)} %copy-done.2, bf16[512,768]{1,0:T(8,128)(2,1)S(1)} %copy.14, s32[4,128]{1,0:T(4,128)S(1)} %multiply_add_fusion, s32[768]{0:T(1024)S(1)} %add_select_fusion.2), kind=kOutput, calls=%fused_computation.6 | convolution fusion | flops 809369600 | bytes 3412992 | tf_op jit(solution)/shard_map/dot_general | solution.py:417
  11.2 0.0 copy-done.1
  11.2 1.1 compare_convert_fusion.place_ref
  12.3 121.8 %shard_map.95 = (f32[768,512]{1,0:T(8,128)}, f32[48,256]{1,0:T(8,128)}) custom-call(bf16[4,256,512]{2,1,0:T(8,128)(2,1)} %bitcast.29, bf16[2,16,512,512]{3,2,1,0:T(8,128)(2,1)} %bitcast.26, bf16[4,768,128]{2,1,0:T(8,128)(2,1)} %compare_convert_fusion.place_ref, f32[2]{0:T(128)} %copy-done.1, s32[1]{0:T(128)} %bitcast.9.own_ref, f32[48,256]{1,0:T(8,128)} %fusion.15.dinv_ref), custom_call_target="tpu_custom_call" | custom-call | tf_op jit(solution)/shard_map/pallas_call | solution.py:436
  134.2 0.0 copy-start
  134.2 3.0 %copy.15 = f32[512,768]{1,0:T(8,128)} copy(f32[512,768]{0,1:T(8,128)} %bitcast.28) | data formatting | bytes 3145728
  137.2 0.0 copy-done
  137.2 0.6 copy.19
  (5 shorter events, 0.0 us)
Async XLA Ops:
  0.6 8.5 %copy-start.2 = (bf16[1,2,512,768]{3,2,1,0:T(8,128)(2,1)S(1)}, bf16[1,2,512,768]{3,2,1,0:T(8,128)(2,1)}, u32[]{:S(2)}) copy-start(bf16[1,2,512,768]{3,2,1,0:T(8,128)(2,1)} %param.9) | copy-start | bytes 4718596
  2.2 9.0 %copy-start.1 = (f32[2]{0:T(128)}, f32[2]{0:T(128)S(1)}, u32[]{:S(2)}) copy-start(f32[2]{0:T(128)S(1)} %select_reduce_fusion.2.weight_ref) | copy-start | bytes 28
  134.2 3.0 %copy-start = (f32[48,256]{1,0:T(8,128)S(1)}, f32[48,256]{1,0:T(8,128)}, u32[]{:S(2)}) copy-start(f32[48,256]{1,0:T(8,128)} %get-tuple-element.19) | copy-start | bytes 147460

commit v2 on v1

--- a/solution.py
+++ b/solution.py
@@ -22,14 +22,18 @@
 
 def kernel(
     dims,
-    piece_ref,
+    factor_ref,
     inv_ref,
-    place_ref,
-    weight_ref,
-    own_ref,
     dinv_ref,
+    widths_ref,
+    pattern_ref,
+    owner_ref,
+    assign_ref,
+    weights_ref,
     panel_ref,
     diag_ref,
+    factor,
+    place_ref,
     pieces,
     inv,
     acc,
@@ -41,6 +45,7 @@
     half_sum,
     parts,
     totals,
+    factor_sem,
     inv_sem,
     recv,
     sz,
@@ -94,9 +99,32 @@
                 barrier, inc=1, device_id=(p, row, z), device_id_type=MESH
             )
 
+    fetch = pltpu.make_async_copy(factor_ref, factor, factor_sem)
+    fetch.start()
     load = pltpu.make_async_copy(inv_ref, inv, inv_sem)
     load.start()
-    pieces[:, pl.ds(me, 1)] = piece_ref[...][:, None]
+
+    live = chunks * width
+    local_width = factor.shape[1]
+    starts = [jnp.int32(0)]
+    for k in range(1, blocks_k):
+        starts.append(starts[-1] + widths_ref[k - 1])
+    slot = lax.broadcasted_iota(jnp.int32, (live, block), 0)
+    position = lax.broadcasted_iota(jnp.int32, (live, block), 1)
+
+    fetch.wait()
+    for i in range(local_width // block):
+        rows = slice(i * block, (i + 1) * block)
+        found = [jnp.zeros((live, block), F32)] * 2
+        for k in range(blocks_k):
+            kept = widths_ref[k] * pattern_ref[me * (local_width // block) + i, k]
+            hit = (slot == position + starts[k]) & (position < kept)
+            pick = jnp.where(hit, 1.0, 0.0).astype(BF16)
+            for part in range(2):
+                found[part] += dot_nt(pick, factor[part, rows, k * block : (k + 1) * block])
+        for part in range(2):
+            packed = found[part].astype(BF16).reshape(chunks, width, block)
+            pieces[:, me, part * width : (part + 1) * width, rows] = packed
     pl.semaphore_wait(barrier, 1 + (2 * zs - 1) + (poles - 1))
 
     def send(c, q, send_sem, to_row, to_col):
@@ -109,11 +137,11 @@
             device_id_type=MESH,
         )
 
-    def up(c, zz):
-        return send(c, at(hi, lo, zz), sz.at[c, zz, 1], row, z + 1)
-
-    def down(c, zz):
-        return send(c, at(hi, lo, zz), sz.at[c, zz, 0], row, z - 1)
+    def up(c, h, zz):
+        return send(c, at(h, lo, zz), sz.at[c, h, zz, 1], row, z + 1)
+
+    def down(c, h, zz):
+        return send(c, at(h, lo, zz), sz.at[c, h, zz, 0], row, z - 1)
 
     def cross(c, zz):
         return send(c, at(hi, lo, zz), sx.at[c, zz], across, z)
@@ -124,28 +152,42 @@
     def arrived(c, q):
         send(c, q, sx.at[0, 0], across, z).wait_recv()
 
+    def early(c, zz):
+        return ((zz == 0) | (zz == zs - 1)) & (c % 2 == 1)
+
     def goes_up(zz):
         return (zz <= z) & (z < zs - 1)
 
     def goes_down(zz):
         return (zz >= z) & (z > 0)
 
-    def forward(c, zz):
-        cross(c, zz).start()
-
+    def crosses(c, zz):
+        return (zz == z) | jnp.logical_not(early(c, zz))
+
+    def forward(c, h, zz):
         @pl.when(goes_up(zz))
         def _():
-            up(c, zz).start()
+            up(c, h, zz).start()
 
         @pl.when(goes_down(zz))
         def _():
-            down(c, zz).start()
-
-        over(c, hi, zz).start()
+            down(c, h, zz).start()
+
+        over(c, h, zz).start()
 
     @pl.loop(0, chunks)
     def _(c):
-        forward(c, z)
+        cross(c, z).start()
+        forward(c, hi, z)
+
+    source = lax.broadcasted_iota(jnp.int32, (block, width), 0)
+    target = lax.broadcasted_iota(jnp.int32, (block, width), 1)
+
+    @pl.loop(0, chunks)
+    def _(c):
+        for k in range(blocks_k):
+            hit = (target + c * width == source + starts[k]) & (source < widths_ref[k])
+            place_ref[c, k * block : (k + 1) * block] = jnp.where(hit, 1.0, 0.0).astype(BF16)
 
     acc[...] = jnp.zeros_like(acc)
     xe[...] = jnp.zeros_like(xe)
@@ -171,20 +213,34 @@
                 visit(zz)
 
     def along(c):
-        compute(c, me)
-
         def visit(zz):
-            arrived(c, at(hi, lo, zz))
-            forward(c, zz)
+            @pl.when(zz != z)
+            def _():
+                arrived(c, at(hi, lo, zz))
+
+                @pl.when(crosses(c, zz))
+                def _():
+                    cross(c, zz).start()
+
+                forward(c, hi, zz)
+
             compute(c, at(hi, lo, zz))
 
-        by_distance(visit, 2)
+            @pl.when(early(c, zz))
+            def _():
+                arrived(c, at(1 - hi, lo, zz))
+                forward(c, 1 - hi, zz)
+                compute(c, at(1 - hi, lo, zz))
+
+        by_distance(visit, 0)
 
     def crossed(c):
         def visit(zz):
-            arrived(c, at(1 - hi, lo, zz))
-            over(c, 1 - hi, zz).start()
-            compute(c, at(1 - hi, lo, zz))
+            @pl.when(jnp.logical_not(early(c, zz)))
+            def _():
+                arrived(c, at(1 - hi, lo, zz))
+                over(c, 1 - hi, zz).start()
+                compute(c, at(1 - hi, lo, zz))
 
         by_distance(visit, 0)
 
@@ -215,8 +271,8 @@
             device_id_type=MESH,
         )
 
-    wr = weight_ref[0]
-    wi = weight_ref[1]
+    wr = weights_ref[assign_ref[0], 0]
+    wi = weights_ref[assign_ref[0], 1]
 
     def others(visit):
         @pl.loop(0, poles)
@@ -239,12 +295,14 @@
         total = shares[c, 0]
         for p in range(1, poles):
             total = total + shares[c, p]
+        total = total.T
         top = total.astype(BF16)
         rest = total - top.astype(F32)
         middle = rest.astype(BF16)
         low = (rest - middle.astype(F32)).astype(BF16)
         place = place_ref[c]
-        panel_ref[...] += dot(place, top) + dot(place, middle) + dot(place, low)
+        terms = jnp.concatenate([top, middle, low], axis=1)
+        panel_ref[...] += dot_nt(terms, jnp.concatenate([place] * 3, axis=1))
 
     @pl.loop(0, chunks + 2)
     def _(t):
@@ -264,7 +322,7 @@
 
     @pl.loop(0, chunks)
     def _(c):
-        lt = pieces[c, own_ref[0]]
+        lt = pieces[c, owner_ref[me]]
         place = place_ref[c]
         le[0] += dot(place, lt[:width]).astype(BF16)
         le[1] += dot(place, lt[width:]).astype(BF16)
@@ -337,7 +395,8 @@
     total = parts[0]
     for j in range(1, 2 * zs):
         total = total + parts[j]
-    totals[pole] = dinv_ref[...] - total
+    dinv = dinv_ref[...].astype(F32)
+    totals[pole] = (wr * dinv[1] + wi * dinv[0]) - total
 
     def result(p, slot):
         return pltpu.make_async_remote_copy(
@@ -355,17 +414,23 @@
     def _(c):
         @pl.loop(0, zs)
         def _(zz):
-            cross(c, zz).wait_send()
             over(c, 0, zz).wait_send()
             over(c, 1, zz).wait_send()
 
-            @pl.when(goes_up(zz))
-            def _():
-                up(c, zz).wait_send()
-
-            @pl.when(goes_down(zz))
-            def _():
-                down(c, zz).wait_send()
+            @pl.when(crosses(c, zz))
+            def _():
+                cross(c, zz).wait_send()
+
+            for h in range(2):
+                travels = (h == hi) | early(c, zz)
+
+                @pl.when(travels & goes_up(zz))
+                def _():
+                    up(c, h, zz).wait_send()
+
+                @pl.when(travels & goes_down(zz))
+                def _():
+                    down(c, h, zz).wait_send()
 
         others(lambda p: share(c, p).wait_send())
 
@@ -386,7 +451,6 @@
     rows_n = lax.axis_size("row")
     assert rows_n == 4
     devices = rows_n * zs
-    device = lax.axis_index(("row", "col"))
     local_width = factor.shape[2]
     total_cols = factor.shape[3]
     db = diag_inverse.shape[2]
@@ -396,52 +460,22 @@
     width = 128
     chunks = live // width
 
-    col_ids = jnp.arange(total_cols, dtype=jnp.int32)
-    col_block = col_ids // block
-    col_pos = col_ids % block
-    block_ids = jnp.arange(blocks_k, dtype=jnp.int32)
-    same = col_block[:, None] == block_ids[None, :]
-    before = block_ids[None, :] < col_block[:, None]
-    col_width = jnp.sum(jnp.where(same, widths[None, :], 0), axis=1)
-    col_start = jnp.sum(jnp.where(before, widths[None, :], 0), axis=1)
-    target = jnp.where(col_pos < col_width, col_start + col_pos, -1)
-    place = (target[:, None] == jnp.arange(live, dtype=jnp.int32)[None, :]).astype(BF16)
-
-    row_block = (device * local_width + jnp.arange(local_width, dtype=jnp.int32)) // block
-    row_onehot = (
-        row_block[:, None] == jnp.arange(pattern.shape[0], dtype=jnp.int32)[None, :]
-    ).astype(F32)
-    row_mask = jnp.dot(row_onehot, pattern.astype(F32), precision=lax.Precision.HIGHEST)
-    mask = jnp.repeat(row_mask, block, axis=1).astype(BF16)
-    masked = factor[0] * mask[None]
-    packed = lax.dot_general(
-        place.reshape(total_cols, chunks, width),
-        masked,
-        (((0,), (2,)), ((), ())),
-        preferred_element_type=F32,
-    ).astype(BF16)
-    packed = packed.transpose(0, 2, 1, 3).reshape(chunks, 2 * width, local_width)
-
-    pole_onehot = assign[0] == jnp.arange(pole_weights.shape[0], dtype=jnp.int32)
-    weight = jnp.sum(jnp.where(pole_onehot[:, None], pole_weights, 0.0), axis=0)
-    own = jnp.sum(jnp.where(jnp.arange(devices, dtype=jnp.int32) == device, owner, 0))
-    inverse_diag = diag_inverse[0].astype(F32)
-    dinv = weight[0] * inverse_diag[1] + weight[1] * inverse_diag[0]
-    places = place.reshape(total_cols, chunks, width).transpose(1, 0, 2)
-
     dims = (chunks, zs, poles, width, blocks_k, block, db)
     vmem = pl.BlockSpec(memory_space=pltpu.VMEM)
+    hbm = pl.BlockSpec(memory_space=pl.ANY)
     smem = pl.BlockSpec(memory_space=pltpu.SMEM)
     dma = pltpu.SemaphoreType.DMA
-    panel, diag = pl.pallas_call(
+    return pl.pallas_call(
         functools.partial(kernel, dims),
         out_shape=(
-            jax.ShapeDtypeStruct((total_cols, local_width), F32),
+            jax.ShapeDtypeStruct((local_width, total_cols), F32),
             jax.ShapeDtypeStruct((db, block), F32),
         ),
-        in_specs=[vmem, pl.BlockSpec(memory_space=pl.ANY), vmem, smem, smem, vmem],
+        in_specs=[hbm, hbm, vmem, smem, smem, smem, smem, smem],
         out_specs=(vmem, vmem),
         scratch_shapes=[
+            pltpu.VMEM((2, local_width, total_cols), BF16),
+            pltpu.VMEM((chunks, total_cols, width), BF16),
             pltpu.VMEM((chunks, devices, 2 * width, local_width), BF16),
             pltpu.VMEM((2, devices, local_width, local_width), BF16),
             pltpu.VMEM((chunks, 2 * width, local_width), F32),
@@ -454,8 +488,9 @@
             pltpu.VMEM((2 * zs, db, block), F32),
             pltpu.VMEM((poles, db, block), F32),
             dma,
+            dma,
             dma((chunks, devices)),
-            dma((chunks, zs, 2)),
+            dma((chunks, 2, zs, 2)),
             dma((chunks, zs)),
             dma((chunks, 2, zs)),
             dma((chunks, poles)),
@@ -471,14 +506,15 @@
             collective_id=0, has_side_effects=True, vmem_limit_bytes=60 * 1024 * 1024
         ),
     )(
-        packed,
+        factor[0],
         inverse[0].reshape(2, devices, local_width, local_width),
-        places,
-        weight,
-        own.reshape(1),
-        dinv,
+        diag_inverse[0],
+        widths,
+        pattern,
+        owner,
+        assign,
+        pole_weights,
     )
-    return panel.T, diag
 
 
 def solution(mesh):

time: 138 us -> 149 us (1.080)
  the two profiles are of different devices: /device:TPU:2 before, /device:TPU:26 now
where the time goes in v2:
time: 149 us
  Pallas kernels  142 us (95%)
  local copies, waits for them, and re-layouts  6.02 us (4%)
    pallas_call x1, Pallas kernels, local(): pl.pallas_call(functools.partial(kernel, dims), out_shape=(jax.ShapeDtype...  142 us
    unnamed x6, local copies, waits for them, and re-layouts  6.02 us

profile of v2, /device:TPU:26, one launch (start us, length us, event | category | flops | bytes accessed | tf_op | source)
XLA Modules:
  0.0 149.1 jit_solution(16241251973648273924)
XLA Ops:
  1.3 1.4 copy.11.weights_ref
  2.6 1.4 copy.10.pattern_ref
  4.0 141.8 %shard_map.95 = (f32[512,768]{1,0:T(8,128)}, f32[48,256]{1,0:T(8,128)}) custom-call(bf16[2,512,768]{2,1,0:T(8,128)(2,1)} %bitcast.4, bf16[2,16,512,512]{3,2,1,0:T(8,128)(2,1)} %bitcast.3, bf16[2,48,256]{2,1,0:T(8,128)(2,1)} %bitcast.5, s32[3]{0:T(128)} %widths_ref.1, s32[32,3]{1,0:T(8,128)} %copy.10.pattern_ref, s32[16]{0:T(128)} %owner_ref.1, ...), custom_call_target="tpu_custom_call" | custom-call | tf_op jit(solution)/shard_map/pallas_call | solution.py:468
  145.8 0.0 copy-start
  145.8 2.7 %copy.15 = f32[512,768]{1,0:T(8,128)} copy(f32[512,768]{1,0:T(8,128)} %get-tuple-element.4) | data formatting | bytes 3145728
  148.5 0.0 copy-done
  148.5 0.6 copy.16
Async XLA Ops:
  145.8 2.7 %copy-start = (f32[48,256]{1,0:T(8,128)S(1)}, f32[48,256]{1,0:T(8,128)}, u32[]{:S(2)}) copy-start(f32[48,256]{1,0:T(8,128)} %get-tuple-element.5) | copy-start | bytes 147460

commit v3 on v2

--- a/solution.py
+++ b/solution.py
@@ -116,8 +116,9 @@
     for i in range(local_width // block):
         rows = slice(i * block, (i + 1) * block)
         found = [jnp.zeros((live, block), F32)] * 2
+        kinds = pattern_ref[pl.ds(me * (local_width // block) + i, 1), :]
         for k in range(blocks_k):
-            kept = widths_ref[k] * pattern_ref[me * (local_width // block) + i, k]
+            kept = widths_ref[k] * kinds[:, k : k + 1]
             hit = (slot == position + starts[k]) & (position < kept)
             pick = jnp.where(hit, 1.0, 0.0).astype(BF16)
             for part in range(2):
@@ -152,17 +153,11 @@
     def arrived(c, q):
         send(c, q, sx.at[0, 0], across, z).wait_recv()
 
-    def early(c, zz):
-        return ((zz == 0) | (zz == zs - 1)) & (c % 2 == 1)
-
     def goes_up(zz):
         return (zz <= z) & (z < zs - 1)
 
     def goes_down(zz):
         return (zz >= z) & (z > 0)
-
-    def crosses(c, zz):
-        return (zz == z) | jnp.logical_not(early(c, zz))
 
     def forward(c, h, zz):
         @pl.when(goes_up(zz))
@@ -175,10 +170,12 @@
 
         over(c, h, zz).start()
 
-    @pl.loop(0, chunks)
-    def _(c):
+    def begin(c):
         cross(c, z).start()
         forward(c, hi, z)
+
+    for c in range(min(2, chunks)):
+        begin(c)
 
     source = lax.broadcasted_iota(jnp.int32, (block, width), 0)
     target = lax.broadcasted_iota(jnp.int32, (block, width), 1)
@@ -201,55 +198,6 @@
         v = dot(lt, inv[1, q])
         acc[c, :width] += u[:width] - v[width:]
         acc[c, width:] += u[width:] + v[:width]
-
-    def by_distance(visit, first):
-        @pl.loop(first, 2 * zs)
-        def _(j):
-            s = j // 2
-            zz = jnp.where(j % 2 == 0, z - s, z + s)
-
-            @pl.when((zz >= 0) & (zz < zs) & (j != 1))
-            def _():
-                visit(zz)
-
-    def along(c):
-        def visit(zz):
-            @pl.when(zz != z)
-            def _():
-                arrived(c, at(hi, lo, zz))
-
-                @pl.when(crosses(c, zz))
-                def _():
-                    cross(c, zz).start()
-
-                forward(c, hi, zz)
-
-            compute(c, at(hi, lo, zz))
-
-            @pl.when(early(c, zz))
-            def _():
-                arrived(c, at(1 - hi, lo, zz))
-                forward(c, 1 - hi, zz)
-                compute(c, at(1 - hi, lo, zz))
-
-        by_distance(visit, 0)
-
-    def crossed(c):
-        def visit(zz):
-            @pl.when(jnp.logical_not(early(c, zz)))
-            def _():
-                arrived(c, at(1 - hi, lo, zz))
-                over(c, 1 - hi, zz).start()
-                compute(c, at(1 - hi, lo, zz))
-
-        by_distance(visit, 0)
-
-    def from_sibling(c, h):
-        def visit(zz):
-            arrived(c, at(h, 1 - lo, zz))
-            compute(c, at(h, 1 - lo, zz))
-
-        by_distance(visit, 0)
 
     def share(c, p):
         return pltpu.make_async_remote_copy(
@@ -271,8 +219,10 @@
             device_id_type=MESH,
         )
 
-    wr = weights_ref[assign_ref[0], 0]
-    wi = weights_ref[assign_ref[0], 1]
+    chosen = lax.broadcasted_iota(jnp.int32, weights_ref.shape, 0) == assign_ref[0]
+    weight = jnp.sum(jnp.where(chosen, weights_ref[...], 0.0), axis=0, keepdims=True)
+    wr = weight[:, 0:1]
+    wi = weight[:, 1:2]
 
     def others(visit):
         @pl.loop(0, poles)
@@ -306,19 +256,40 @@
 
     @pl.loop(0, chunks + 2)
     def _(t):
+        @pl.when(t < chunks - 2)
+        def _():
+            begin(t + 2)
+
+        @pl.loop(0, 2 * zs)
+        def _(j):
+            s = j // 2
+            zz = jnp.where(j % 2 == 0, z - s, z + s)
+
+            @pl.when((zz >= 0) & (zz < zs) & (j != 1))
+            def _():
+                @pl.when((t < chunks) & (zz != z))
+                def _():
+                    arrived(t, at(hi, lo, zz))
+                    cross(t, zz).start()
+                    forward(t, hi, zz)
+
+                @pl.when((t >= 1) & (t <= chunks))
+                def _():
+                    arrived(t - 1, at(1 - hi, lo, zz))
+                    over(t - 1, 1 - hi, zz).start()
+                    compute(t - 1, at(hi, lo, zz))
+                    arrived(t - 1, at(hi, 1 - lo, zz))
+                    compute(t - 1, at(hi, 1 - lo, zz))
+                    compute(t - 1, at(1 - hi, lo, zz))
+
+                @pl.when(t >= 2)
+                def _():
+                    arrived(t - 2, at(1 - hi, 1 - lo, zz))
+                    compute(t - 2, at(1 - hi, 1 - lo, zz))
+
         @pl.when(t >= 2)
         def _():
-            from_sibling(t - 2, 1 - hi)
             finish(t - 2)
-
-        @pl.when(t < chunks)
-        def _():
-            along(t)
-
-        @pl.when((t >= 1) & (t <= chunks))
-        def _():
-            from_sibling(t - 1, hi)
-            crossed(t - 1)
 
     @pl.loop(0, chunks)
     def _(c):
@@ -417,20 +388,15 @@
             over(c, 0, zz).wait_send()
             over(c, 1, zz).wait_send()
 
-            @pl.when(crosses(c, zz))
+            cross(c, zz).wait_send()
+
+            @pl.when(goes_up(zz))
             def _():
-                cross(c, zz).wait_send()
-
-            for h in range(2):
-                travels = (h == hi) | early(c, zz)
-
-                @pl.when(travels & goes_up(zz))
-                def _():
-                    up(c, h, zz).wait_send()
-
-                @pl.when(travels & goes_down(zz))
-                def _():
-                    down(c, h, zz).wait_send()
+                up(c, hi, zz).wait_send()
+
+            @pl.when(goes_down(zz))
+            def _():
+                down(c, hi, zz).wait_send()
 
         others(lambda p: share(c, p).wait_send())
 
@@ -471,7 +437,7 @@
             jax.ShapeDtypeStruct((local_width, total_cols), F32),
             jax.ShapeDtypeStruct((db, block), F32),
         ),
-        in_specs=[hbm, hbm, vmem, smem, smem, smem, smem, smem],
+        in_specs=[hbm, hbm, vmem, smem, vmem, smem, smem, vmem],
         out_specs=(vmem, vmem),
         scratch_shapes=[
             pltpu.VMEM((2, local_width, total_cols), BF16),

time: 149 us -> 131 us (0.88)
  the two profiles are of different devices: /device:TPU:26 before, /device:TPU:2 now
where the time goes in v3:
time: 131 us
  Pallas kernels  124 us (95%)
  local copies, waits for them, and re-layouts  6.02 us (5%)
    pallas_call x1, Pallas kernels, local(): pl.pallas_call(functools.partial(kernel, dims), out_shape=(jax.ShapeDtype...  124 us
    unnamed x6, local copies, waits for them, and re-layouts  6.02 us

profile of v3, /device:TPU:2, one launch (start us, length us, event | category | flops | bytes accessed | tf_op | source)
XLA Modules:
  0.0 131.2 jit_solution(7233171484121367777)
XLA Ops:
  1.3 1.4 %copy.11.weights_ref = f32[20,2]{1,0:T(8,128)} copy(f32[20,2]{0,1:T(2,128)} %param.15) | data formatting | bytes 320 | tf_op args[7]
  2.6 1.4 %copy.10.pattern_ref = s32[32,3]{1,0:T(8,128)} copy(s32[32,3]{0,1:T(4,128)} %param.12) | data formatting | bytes 768 | tf_op args[4]
  4.0 123.9 %shard_map.95 = (f32[512,768]{1,0:T(8,128)}, f32[48,256]{1,0:T(8,128)}) custom-call(bf16[2,512,768]{2,1,0:T(8,128)(2,1)} %bitcast.4, bf16[2,16,512,512]{3,2,1,0:T(8,128)(2,1)} %bitcast.3, bf16[2,48,256]{2,1,0:T(8,128)(2,1)} %bitcast.5, s32[3]{0:T(128)} %widths_ref.1, s32[32,3]{1,0:T(8,128)} %copy.10.pattern_ref, s32[16]{0:T(128)} %owner_ref.1, ...), custom_call_target="tpu_custom_call" | custom-call | tf_op jit(solution)/shard_map/pallas_call | solution.py:434
  127.9 0.0 copy-start
  127.9 2.7 %copy.15 = f32[512,768]{1,0:T(8,128)} copy(f32[512,768]{1,0:T(8,128)} %get-tuple-element.4) | data formatting | bytes 3145728
  130.6 0.0 copy-done
  130.6 0.6 copy.16
Async XLA Ops:
  127.9 2.7 %copy-start = (f32[48,256]{1,0:T(8,128)S(1)}, f32[48,256]{1,0:T(8,128)}, u32[]{:S(2)}) copy-start(f32[48,256]{1,0:T(8,128)} %get-tuple-element.5) | copy-start | bytes 147460

commit v4 on v3

--- a/solution.py
+++ b/solution.py
@@ -49,6 +49,7 @@
     inv_sem,
     recv,
     sz,
+    sd,
     sx,
     sc,
     ys,
@@ -116,9 +117,11 @@
     for i in range(local_width // block):
         rows = slice(i * block, (i + 1) * block)
         found = [jnp.zeros((live, block), F32)] * 2
-        kinds = pattern_ref[pl.ds(me * (local_width // block) + i, 1), :]
+        here = lax.broadcasted_iota(jnp.int32, pattern_ref.shape, 1)
+        here = here == me * (local_width // block) + i
+        kinds = jnp.sum(jnp.where(here, pattern_ref[...], 0), axis=1, keepdims=True)
         for k in range(blocks_k):
-            kept = widths_ref[k] * kinds[:, k : k + 1]
+            kept = widths_ref[k] * kinds[k : k + 1]
             hit = (slot == position + starts[k]) & (position < kept)
             pick = jnp.where(hit, 1.0, 0.0).astype(BF16)
             for part in range(2):
@@ -138,11 +141,14 @@
             device_id_type=MESH,
         )
 
-    def up(c, h, zz):
-        return send(c, at(h, lo, zz), sz.at[c, h, zz, 1], row, z + 1)
-
-    def down(c, h, zz):
-        return send(c, at(h, lo, zz), sz.at[c, h, zz, 0], row, z - 1)
+    def up(c, zz):
+        return send(c, at(hi, lo, zz), sz.at[c, zz, 1], row, z + 1)
+
+    def down(c, zz):
+        return send(c, at(hi, lo, zz), sz.at[c, zz, 0], row, z - 1)
+
+    def straight(c, zz):
+        return send(c, me, sd.at[c, zz], row, zz)
 
     def cross(c, zz):
         return send(c, at(hi, lo, zz), sx.at[c, zz], across, z)
@@ -153,29 +159,40 @@
     def arrived(c, q):
         send(c, q, sx.at[0, 0], across, z).wait_recv()
 
+    def inner(zz):
+        return (zz > 0) & (zz < zs - 1)
+
     def goes_up(zz):
-        return (zz <= z) & (z < zs - 1)
+        return inner(zz) & (zz <= z) & (z < zs - 1)
 
     def goes_down(zz):
-        return (zz >= z) & (z > 0)
-
-    def forward(c, h, zz):
+        return inner(zz) & (zz >= z) & (z > 0)
+
+    def along(visit_up, visit_down, zz):
         @pl.when(goes_up(zz))
         def _():
-            up(c, h, zz).start()
+            visit_up()
 
         @pl.when(goes_down(zz))
         def _():
-            down(c, h, zz).start()
-
-        over(c, h, zz).start()
-
-    def begin(c):
-        cross(c, z).start()
-        forward(c, hi, z)
-
-    for c in range(min(2, chunks)):
-        begin(c)
+            visit_down()
+
+    def from_end(visit):
+        @pl.when(jnp.logical_not(inner(z)))
+        def _():
+            @pl.loop(1, zs)
+            def _(s):
+                visit(jnp.where(z == 0, s, zs - 1 - s))
+
+    def forward(c, zz):
+        along(lambda: up(c, zz).start(), lambda: down(c, zz).start(), zz)
+        cross(c, zz).start()
+        over(c, hi, zz).start()
+
+    @pl.loop(0, chunks)
+    def _(c):
+        from_end(lambda zz: straight(c, zz).start())
+        forward(c, z)
 
     source = lax.broadcasted_iota(jnp.int32, (block, width), 0)
     target = lax.broadcasted_iota(jnp.int32, (block, width), 1)
@@ -219,10 +236,10 @@
             device_id_type=MESH,
         )
 
-    chosen = lax.broadcasted_iota(jnp.int32, weights_ref.shape, 0) == assign_ref[0]
-    weight = jnp.sum(jnp.where(chosen, weights_ref[...], 0.0), axis=0, keepdims=True)
-    wr = weight[:, 0:1]
-    wi = weight[:, 1:2]
+    chosen = lax.broadcasted_iota(jnp.int32, weights_ref.shape, 1) == assign_ref[0]
+    weight = jnp.sum(jnp.where(chosen, weights_ref[...], 0.0), axis=1, keepdims=True)
+    wr = weight[0:1]
+    wi = weight[1:2]
 
     def others(visit):
         @pl.loop(0, poles)
@@ -256,10 +273,6 @@
 
     @pl.loop(0, chunks + 2)
     def _(t):
-        @pl.when(t < chunks - 2)
-        def _():
-            begin(t + 2)
-
         @pl.loop(0, 2 * zs)
         def _(j):
             s = j // 2
@@ -267,17 +280,19 @@
 
             @pl.when((zz >= 0) & (zz < zs) & (j != 1))
             def _():
-                @pl.when((t < chunks) & (zz != z))
+                @pl.when(t < chunks)
                 def _():
-                    arrived(t, at(hi, lo, zz))
-                    cross(t, zz).start()
-                    forward(t, hi, zz)
+                    @pl.when(zz != z)
+                    def _():
+                        arrived(t, at(hi, lo, zz))
+                        forward(t, zz)
+
+                    compute(t, at(hi, lo, zz))
 
                 @pl.when((t >= 1) & (t <= chunks))
                 def _():
                     arrived(t - 1, at(1 - hi, lo, zz))
                     over(t - 1, 1 - hi, zz).start()
-                    compute(t - 1, at(hi, lo, zz))
                     arrived(t - 1, at(hi, 1 - lo, zz))
                     compute(t - 1, at(hi, 1 - lo, zz))
                     compute(t - 1, at(1 - hi, lo, zz))
@@ -390,14 +405,9 @@
 
             cross(c, zz).wait_send()
 
-            @pl.when(goes_up(zz))
-            def _():
-                up(c, hi, zz).wait_send()
-
-            @pl.when(goes_down(zz))
-            def _():
-                down(c, hi, zz).wait_send()
-
+            along(lambda: up(c, zz).wait_send(), lambda: down(c, zz).wait_send(), zz)
+
+        from_end(lambda zz: straight(c, zz).wait_send())
         others(lambda p: share(c, p).wait_send())
 
     for h in range(2):
@@ -456,7 +466,8 @@
             dma,
             dma,
             dma((chunks, devices)),
-            dma((chunks, 2, zs, 2)),
+            dma((chunks, zs, 2)),
+            dma((chunks, zs)),
             dma((chunks, zs)),
             dma((chunks, 2, zs)),
             dma((chunks, poles)),
@@ -476,10 +487,10 @@
         inverse[0].reshape(2, devices, local_width, local_width),
         diag_inverse[0],
         widths,
-        pattern,
+        pattern.T,
         owner,
         assign,
-        pole_weights,
+        pole_weights.T,
     )
 
 

time: 131 us -> 140 us (1.069)
  Pallas kernels: 124 us -> 135 us
  local copies, waits for them, and re-layouts: 6.02 us -> 3.29 us
    pallas_call x1, Pallas kernels: 124 us -> 135 us  [local(): pl.pallas_call(functools.partial(kernel, dims), out_shape=(jax.ShapeDtype...]
    unnamed x6 -> x4, local copies, waits for them, and re-layouts: 6.02 us -> 3.29 us
where the time goes in v4:
time: 140 us; the launch traced here: 139 us
  Pallas kernels  135 us (96%)
  local copies, waits for them, and re-layouts  3.29 us (2%)
    pallas_call x1, Pallas kernels, local(): pl.pallas_call(functools.partial(kernel, dims), out_shape=(jax.ShapeDtype...  135 us
    unnamed x4, local copies, waits for them, and re-layouts  3.29 us

profile of v4, /device:TPU:2, one launch (start us, length us, event | category | flops | bytes accessed | tf_op | source)
XLA Modules:
  0.0 139.3 jit_solution(8826812028878762972)
XLA Ops:
  1.3 134.7 %shard_map.95 = (f32[512,768]{1,0:T(8,128)}, f32[48,256]{1,0:T(8,128)}) custom-call(bf16[2,512,768]{2,1,0:T(8,128)(2,1)} %bitcast.6, bf16[2,16,512,512]{3,2,1,0:T(8,128)(2,1)} %bitcast.5, bf16[2,48,256]{2,1,0:T(8,128)(2,1)} %bitcast.7, s32[3]{0:T(128)} %widths_ref.1, s32[3,32]{1,0:T(4,128)} %bitcast.8, s32[16]{0:T(128)} %owner_ref.1, s32[1]{0:T(128)S(6)} %copy.12.assign_ref, ...), custom_call_target="tpu_custom_call" | custom-call | tf_op jit(solution)/shard_map/pallas_call | solution.py:444
  136.0 0.0 copy-start
  136.0 2.7 %copy.13 = f32[512,768]{1,0:T(8,128)} copy(f32[512,768]{1,0:T(8,128)} %get-tuple-element.4) | data formatting | bytes 3145728
  138.7 0.0 copy-done
  138.7 0.6 copy.14
Async XLA Ops:
  136.0 2.7 %copy-start = (f32[48,256]{1,0:T(8,128)S(1)}, f32[48,256]{1,0:T(8,128)}, u32[]{:S(2)}) copy-start(f32[48,256]{1,0:T(8,128)} %get-tuple-element.5) | copy-start | bytes 147460

commit v5 on v4

--- a/solution.py
+++ b/solution.py
@@ -49,7 +49,6 @@
     inv_sem,
     recv,
     sz,
-    sd,
     sx,
     sc,
     ys,
@@ -106,6 +105,7 @@
     load.start()
 
     live = chunks * width
+    lt_width = inv.shape[3]
     local_width = factor.shape[1]
     starts = [jnp.int32(0)]
     for k in range(1, blocks_k):
@@ -147,9 +147,6 @@
     def down(c, zz):
         return send(c, at(hi, lo, zz), sz.at[c, zz, 0], row, z - 1)
 
-    def straight(c, zz):
-        return send(c, me, sd.at[c, zz], row, zz)
-
     def cross(c, zz):
         return send(c, at(hi, lo, zz), sx.at[c, zz], across, z)
 
@@ -159,14 +156,11 @@
     def arrived(c, q):
         send(c, q, sx.at[0, 0], across, z).wait_recv()
 
-    def inner(zz):
-        return (zz > 0) & (zz < zs - 1)
-
     def goes_up(zz):
-        return inner(zz) & (zz <= z) & (z < zs - 1)
+        return (zz <= z) & (z < zs - 1)
 
     def goes_down(zz):
-        return inner(zz) & (zz >= z) & (z > 0)
+        return (zz >= z) & (z > 0)
 
     def along(visit_up, visit_down, zz):
         @pl.when(goes_up(zz))
@@ -177,13 +171,6 @@
         def _():
             visit_down()
 
-    def from_end(visit):
-        @pl.when(jnp.logical_not(inner(z)))
-        def _():
-            @pl.loop(1, zs)
-            def _(s):
-                visit(jnp.where(z == 0, s, zs - 1 - s))
-
     def forward(c, zz):
         along(lambda: up(c, zz).start(), lambda: down(c, zz).start(), zz)
         cross(c, zz).start()
@@ -191,7 +178,6 @@
 
     @pl.loop(0, chunks)
     def _(c):
-        from_end(lambda zz: straight(c, zz).start())
         forward(c, z)
 
     source = lax.broadcasted_iota(jnp.int32, (block, width), 0)
@@ -209,12 +195,13 @@
     panel_ref[...] = jnp.zeros_like(panel_ref)
     load.wait()
 
-    def compute(c, q):
-        lt = pieces[c, q]
-        u = dot(lt, inv[0, q])
-        v = dot(lt, inv[1, q])
-        acc[c, :width] += u[:width] - v[width:]
-        acc[c, width:] += u[width:] + v[:width]
+    def compute(pair, q):
+        some = pl.ds(2 * pair, 2)
+        lt = pieces[some, q].reshape(4 * width, lt_width)
+        u = dot(lt, inv[0, q]).reshape(2, 2 * width, lt_width)
+        v = dot(lt, inv[1, q]).reshape(2, 2 * width, lt_width)
+        acc[some, :width] += u[:, :width] - v[:, width:]
+        acc[some, width:] += u[:, width:] + v[:, :width]
 
     def share(c, p):
         return pltpu.make_async_remote_copy(
@@ -271,40 +258,54 @@
         terms = jnp.concatenate([top, middle, low], axis=1)
         panel_ref[...] += dot_nt(terms, jnp.concatenate([place] * 3, axis=1))
 
-    @pl.loop(0, chunks + 2)
-    def _(t):
-        @pl.loop(0, 2 * zs)
-        def _(j):
-            s = j // 2
-            zz = jnp.where(j % 2 == 0, z - s, z + s)
-
-            @pl.when((zz >= 0) & (zz < zs) & (j != 1))
-            def _():
-                @pl.when(t < chunks)
+    pairs = chunks // 2
+    slots = pairs * zs
+    near, far = 2, 3
+
+    @pl.loop(0, slots + far)
+    def _(n):
+        @pl.loop(0, 2)
+        def _(side):
+            def visit(m, body):
+                s = m // pairs
+                zz = jnp.where(side == 0, z - s, z + s)
+                inside = (m >= 0) & (m < slots) & (zz >= 0) & (zz < zs)
+
+                @pl.when(inside & ((s > 0) | (side == 0)))
                 def _():
-                    @pl.when(zz != z)
-                    def _():
-                        arrived(t, at(hi, lo, zz))
-                        forward(t, zz)
-
-                    compute(t, at(hi, lo, zz))
-
-                @pl.when((t >= 1) & (t <= chunks))
+                    body(lax.rem(m, pairs), zz)
+
+            def first(pair, zz):
+                @pl.when(zz != z)
                 def _():
-                    arrived(t - 1, at(1 - hi, lo, zz))
-                    over(t - 1, 1 - hi, zz).start()
-                    arrived(t - 1, at(hi, 1 - lo, zz))
-                    compute(t - 1, at(hi, 1 - lo, zz))
-                    compute(t - 1, at(1 - hi, lo, zz))
-
-                @pl.when(t >= 2)
-                def _():
-                    arrived(t - 2, at(1 - hi, 1 - lo, zz))
-                    compute(t - 2, at(1 - hi, 1 - lo, zz))
-
-        @pl.when(t >= 2)
+                    for c in (2 * pair, 2 * pair + 1):
+                        arrived(c, at(hi, lo, zz))
+                        forward(c, zz)
+
+                compute(pair, at(hi, lo, zz))
+
+            def second(pair, zz):
+                for c in (2 * pair, 2 * pair + 1):
+                    arrived(c, at(1 - hi, lo, zz))
+                    over(c, 1 - hi, zz).start()
+                    arrived(c, at(hi, 1 - lo, zz))
+                compute(pair, at(hi, 1 - lo, zz))
+                compute(pair, at(1 - hi, lo, zz))
+
+            def third(pair, zz):
+                for c in (2 * pair, 2 * pair + 1):
+                    arrived(c, at(1 - hi, 1 - lo, zz))
+                compute(pair, at(1 - hi, 1 - lo, zz))
+
+            visit(n, first)
+            visit(n - near, second)
+            visit(n - far, third)
+
+        @pl.when(n - far >= slots - pairs)
         def _():
-            finish(t - 2)
+            pair = lax.rem(n - far, pairs)
+            finish(2 * pair)
+            finish(2 * pair + 1)
 
     @pl.loop(0, chunks)
     def _(c):
@@ -407,7 +408,6 @@
 
             along(lambda: up(c, zz).wait_send(), lambda: down(c, zz).wait_send(), zz)
 
-        from_end(lambda zz: straight(c, zz).wait_send())
         others(lambda p: share(c, p).wait_send())
 
     for h in range(2):
@@ -468,7 +468,6 @@
             dma((chunks, devices)),
             dma((chunks, zs, 2)),
             dma((chunks, zs)),
-            dma((chunks, zs)),
             dma((chunks, 2, zs)),
             dma((chunks, poles)),
             dma((chunks, poles)),

time: 140 us -> 138 us (0.986)
  Pallas kernels: 135 us -> 133 us
where the time goes in v5:
time: 138 us
  Pallas kernels  133 us (96%)
  local copies, waits for them, and re-layouts  3.29 us (2%)
    pallas_call x1, Pallas kernels, local(): pl.pallas_call(functools.partial(kernel, dims), out_shape=(jax.ShapeDtype...  133 us
    unnamed x4, local copies, waits for them, and re-layouts  3.29 us

profile of v5, /device:TPU:2, one launch (start us, length us, event | category | flops | bytes accessed | tf_op | source)
XLA Modules:
  0.0 137.9 jit_solution(13409604702259330777)
XLA Ops:
  1.3 133.4 %shard_map.95 = (f32[512,768]{1,0:T(8,128)}, f32[48,256]{1,0:T(8,128)}) custom-call(bf16[2,512,768]{2,1,0:T(8,128)(2,1)} %bitcast.6, bf16[2,16,512,512]{3,2,1,0:T(8,128)(2,1)} %bitcast.5, bf16[2,48,256]{2,1,0:T(8,128)(2,1)} %bitcast.7, s32[3]{0:T(128)} %widths_ref.1, s32[3,32]{1,0:T(4,128)} %bitcast.8, s32[16]{0:T(128)} %owner_ref.1, s32[1]{0:T(128)S(6)} %copy.12.assign_ref, ...), custom_call_target="tpu_custom_call" | custom-call | tf_op jit(solution)/shard_map/pallas_call | solution.py:444
  134.6 0.0 copy-start
  134.7 2.7 %copy.13 = f32[512,768]{1,0:T(8,128)} copy(f32[512,768]{1,0:T(8,128)} %get-tuple-element.4) | data formatting | bytes 3145728
  137.3 0.0 copy-done
  137.3 0.6 copy.14
Async XLA Ops:
  134.6 2.7 %copy-start = (f32[48,256]{1,0:T(8,128)S(1)}, f32[48,256]{1,0:T(8,128)}, u32[]{:S(2)}) copy-start(f32[48,256]{1,0:T(8,128)} %get-tuple-element.5) | copy-start | bytes 147460

commit v6 on v4

--- a/solution.py
+++ b/solution.py
@@ -37,6 +37,7 @@
     pieces,
     inv,
     acc,
+    held,
     shares,
     xe,
     le,
@@ -49,7 +50,6 @@
     inv_sem,
     recv,
     sz,
-    sd,
     sx,
     sc,
     ys,
@@ -147,9 +147,6 @@
     def down(c, zz):
         return send(c, at(hi, lo, zz), sz.at[c, zz, 0], row, z - 1)
 
-    def straight(c, zz):
-        return send(c, me, sd.at[c, zz], row, zz)
-
     def cross(c, zz):
         return send(c, at(hi, lo, zz), sx.at[c, zz], across, z)
 
@@ -159,14 +156,11 @@
     def arrived(c, q):
         send(c, q, sx.at[0, 0], across, z).wait_recv()
 
-    def inner(zz):
-        return (zz > 0) & (zz < zs - 1)
-
     def goes_up(zz):
-        return inner(zz) & (zz <= z) & (z < zs - 1)
+        return (zz <= z) & (z < zs - 1)
 
     def goes_down(zz):
-        return inner(zz) & (zz >= z) & (z > 0)
+        return (zz >= z) & (z > 0)
 
     def along(visit_up, visit_down, zz):
         @pl.when(goes_up(zz))
@@ -176,22 +170,13 @@
         @pl.when(goes_down(zz))
         def _():
             visit_down()
-
-    def from_end(visit):
-        @pl.when(jnp.logical_not(inner(z)))
-        def _():
-            @pl.loop(1, zs)
-            def _(s):
-                visit(jnp.where(z == 0, s, zs - 1 - s))
 
     def forward(c, zz):
         along(lambda: up(c, zz).start(), lambda: down(c, zz).start(), zz)
         cross(c, zz).start()
         over(c, hi, zz).start()
 
-    @pl.loop(0, chunks)
-    def _(c):
-        from_end(lambda zz: straight(c, zz).start())
+    for c in range(min(2, chunks)):
         forward(c, z)
 
     source = lax.broadcasted_iota(jnp.int32, (block, width), 0)
@@ -204,6 +189,7 @@
             place_ref[c, k * block : (k + 1) * block] = jnp.where(hit, 1.0, 0.0).astype(BF16)
 
     acc[...] = jnp.zeros_like(acc)
+    held[...] = jnp.zeros_like(held)
     xe[...] = jnp.zeros_like(xe)
     le[...] = jnp.zeros_like(le)
     panel_ref[...] = jnp.zeros_like(panel_ref)
@@ -211,6 +197,7 @@
 
     def compute(c, q):
         lt = pieces[c, q]
+        held[c] = jnp.where(q == owner_ref[me], lt, held[c])
         u = dot(lt, inv[0, q])
         v = dot(lt, inv[1, q])
         acc[c, :width] += u[:width] - v[width:]
@@ -256,6 +243,8 @@
         place = place_ref[c]
         xe[0] += dot(place, xr.astype(BF16)).astype(BF16)
         xe[1] += dot(place, xi.astype(BF16)).astype(BF16)
+        le[0] += dot(place, held[c, :width]).astype(BF16)
+        le[1] += dot(place, held[c, width:]).astype(BF16)
 
     def receive(c):
         others(lambda p: share_from(c, p).wait_recv())
@@ -273,6 +262,14 @@
 
     @pl.loop(0, chunks + 2)
     def _(t):
+        @pl.when(t < chunks - 2)
+        def _():
+            forward(t + 2, z)
+
+        @pl.when(t >= 4)
+        def _():
+            receive(t - 4)
+
         @pl.loop(0, 2 * zs)
         def _(j):
             s = j // 2
@@ -305,13 +302,6 @@
         @pl.when(t >= 2)
         def _():
             finish(t - 2)
-
-    @pl.loop(0, chunks)
-    def _(c):
-        lt = pieces[c, owner_ref[me]]
-        place = place_ref[c]
-        le[0] += dot(place, lt[:width]).astype(BF16)
-        le[1] += dot(place, lt[width:]).astype(BF16)
 
     for k in range(blocks_k):
         rows = slice(k * block, (k + 1) * block)
@@ -339,9 +329,7 @@
         )
         halves[h].start()
 
-    @pl.loop(0, chunks - 1)
-    def _(c):
-        receive(c)
+    receive(chunks - 2)
 
     for h in range(2):
         halves[h].wait_recv()
@@ -407,7 +395,6 @@
 
             along(lambda: up(c, zz).wait_send(), lambda: down(c, zz).wait_send(), zz)
 
-        from_end(lambda zz: straight(c, zz).wait_send())
         others(lambda p: share(c, p).wait_send())
 
     for h in range(2):
@@ -455,6 +442,7 @@
             pltpu.VMEM((chunks, devices, 2 * width, local_width), BF16),
             pltpu.VMEM((2, devices, local_width, local_width), BF16),
             pltpu.VMEM((chunks, 2 * width, local_width), F32),
+            pltpu.VMEM((chunks, 2 * width, local_width), BF16),
             pltpu.VMEM((chunks, poles, width, local_width), F32),
             pltpu.VMEM((2, total_cols, local_width), BF16),
             pltpu.VMEM((2, total_cols, local_width), BF16),
@@ -467,7 +455,6 @@
             dma,
             dma((chunks, devices)),
             dma((chunks, zs, 2)),
-            dma((chunks, zs)),
             dma((chunks, zs)),
             dma((chunks, 2, zs)),
             dma((chunks, poles)),

time: 140 us -> 127 us (0.907)
  Pallas kernels: 135 us -> 122 us
    pallas_call x1, Pallas kernels: 135 us -> 122 us  [local(): pl.pallas_call(functools.partial(kernel, dims), out_shape=(jax.ShapeDtype...]
where the time goes in v6:
time: 127 us
  Pallas kernels  122 us (96%)
  local copies, waits for them, and re-layouts  3.29 us (3%)
  between operations  1.3 us (1%)
    pallas_call x1, Pallas kernels, local(): pl.pallas_call(functools.partial(kernel, dims), out_shape=(jax.ShapeDtype...  122 us
    unnamed x4, local copies, waits for them, and re-layouts  3.29 us

profile of v6, /device:TPU:2, one launch (start us, length us, event | category | flops | bytes accessed | tf_op | source)
XLA Modules:
  0.0 126.9 jit_solution(7543200254178912481)
XLA Ops:
  1.3 122.3 %shard_map.95 = (f32[512,768]{1,0:T(8,128)}, f32[48,256]{1,0:T(8,128)}) custom-call(bf16[2,512,768]{2,1,0:T(8,128)(2,1)} %bitcast.6, bf16[2,16,512,512]{3,2,1,0:T(8,128)(2,1)} %bitcast.5, bf16[2,48,256]{2,1,0:T(8,128)(2,1)} %bitcast.7, s32[3]{0:T(128)} %widths_ref.1, s32[3,32]{1,0:T(4,128)} %bitcast.8, s32[16]{0:T(128)} %owner_ref.1, s32[1]{0:T(128)S(6)} %copy.12.assign_ref, ...), custom_call_target="tpu_custom_call" | custom-call | tf_op jit(solution)/shard_map/pallas_call | solution.py:431
  123.6 0.0 copy-start
  123.6 2.7 %copy.13 = f32[512,768]{1,0:T(8,128)} copy(f32[512,768]{1,0:T(8,128)} %get-tuple-element.4) | data formatting | bytes 3145728
  126.3 0.0 copy-done
  126.3 0.6 copy.14
Async XLA Ops:
  123.6 2.7 %copy-start = (f32[48,256]{1,0:T(8,128)S(1)}, f32[48,256]{1,0:T(8,128)}, u32[]{:S(2)}) copy-start(f32[48,256]{1,0:T(8,128)} %get-tuple-element.5) | copy-start | bytes 147460

commit v7 on v6

--- a/solution.py
+++ b/solution.py
@@ -176,8 +176,7 @@
         cross(c, zz).start()
         over(c, hi, zz).start()
 
-    for c in range(min(2, chunks)):
-        forward(c, z)
+    forward(0, z)
 
     source = lax.broadcasted_iota(jnp.int32, (block, width), 0)
     target = lax.broadcasted_iota(jnp.int32, (block, width), 1)
@@ -262,9 +261,9 @@
 
     @pl.loop(0, chunks + 2)
     def _(t):
-        @pl.when(t < chunks - 2)
-        def _():
-            forward(t + 2, z)
+        @pl.when(t < chunks - 1)
+        def _():
+            forward(t + 1, z)
 
         @pl.when(t >= 4)
         def _():

time: 127 us -> 127 us (level)
  no operation moved by 1% of the time
where the time goes in v7:
time: 127 us
  Pallas kernels  122 us (96%)
  local copies, waits for them, and re-layouts  3.29 us (3%)
  between operations  1.3 us (1%)
    pallas_call x1, Pallas kernels, local(): pl.pallas_call(functools.partial(kernel, dims), out_shape=(jax.ShapeDtype...  122 us
    unnamed x4, local copies, waits for them, and re-layouts  3.29 us

profile of v7, /device:TPU:2, one launch (start us, length us, event | category | flops | bytes accessed | tf_op | source)
XLA Modules:
  0.0 126.9 jit_solution(6071265983316007928)
XLA Ops:
  1.3 122.3 %shard_map.95 = (f32[512,768]{1,0:T(8,128)}, f32[48,256]{1,0:T(8,128)}) custom-call(bf16[2,512,768]{2,1,0:T(8,128)(2,1)} %bitcast.6, bf16[2,16,512,512]{3,2,1,0:T(8,128)(2,1)} %bitcast.5, bf16[2,48,256]{2,1,0:T(8,128)(2,1)} %bitcast.7, s32[3]{0:T(128)} %widths_ref.1, s32[3,32]{1,0:T(4,128)} %bitcast.8, s32[16]{0:T(128)} %owner_ref.1, s32[1]{0:T(128)S(6)} %copy.12.assign_ref, ...), custom_call_target="tpu_custom_call" | custom-call | tf_op jit(solution)/shard_map/pallas_call | solution.py:430
  123.6 0.0 copy-start
  123.6 2.7 %copy.13 = f32[512,768]{1,0:T(8,128)} copy(f32[512,768]{1,0:T(8,128)} %get-tuple-element.4) | data formatting | bytes 3145728
  126.3 0.0 copy-done
  126.3 0.6 copy.14
Async XLA Ops:
  123.6 2.7 %copy-start = (f32[48,256]{1,0:T(8,128)S(1)}, f32[48,256]{1,0:T(8,128)}, u32[]{:S(2)}) copy-start(f32[48,256]{1,0:T(8,128)} %get-tuple-element.5) | copy-start | bytes 147460
